TPU v7x, 128 devices: a whole 4x4x4 slice. The times are simulated.
128 devices in a mesh: section: 2 (over y_hi), shard: 2 (over core), replica: 32 (over y_lo, z, x).
Axes of the slice: x: 4, y: 4 (y_hi: 2, y_lo: 2; y = y_hi * 2 + y_lo), z: 4, core: 2. Of those that a mesh axis runs over, the one named last changes fastest.
Arguments:
- inputs: bfloat16 [2, 64, 128, 1024], P(None, ('shard', 'replica')), may hold values from -6 to 6
- cotangent: bfloat16 [2, 64, 128, 1024], P(None, ('shard', 'replica')), may hold values from -6 to 6
- segments: int32 [2, 64, 128], P(None, ('shard', 'replica')), may hold values from 0 to 3, never falling along the last dimension, each value on 1 to 64 neighbouring positions
- routes: int32 [2, 2, 64, 128, 2], P('section', None, ('shard', 'replica')), may hold values from 0 to 2, all different within a row; in each aligned block of 128 rows (0 to 127, 128 to 255, ..., all dimensions but the last counted through in order) at most 96 rows name the same one
- mixer_gain: bfloat16 [2, 1024], P('section', 'shard'), may hold values from 0.5 to 1.5
- query_weight: bfloat16 [2, 1024, 1024], P('section', 'shard'), may hold values from -0.25 to 0.25
- key_matrix: bfloat16 [2, 1024, 512], P('section', 'shard'), may hold values from -0.25 to 0.25
- value_matrix: bfloat16 [2, 1024, 512], P('section', 'shard'), may hold values from -0.1875 to 0.1875
- out_weight: bfloat16 [2, 1024, 1024], P('section', 'shard'), may hold values from -0.375 to 0.375
- expert_gain: bfloat16 [2, 1024], P('section', 'shard'), may hold values from 0.5 to 1.5
- router_weight: bfloat16 [2, 1024, 3], P('section', 'shard'), may hold values from -0.125 to 0.125
- gate_weight: bfloat16 [2, 3, 1024, 512], P('section', None, 'shard'), may hold values from -0.1875 to 0.1875
- up_weight: bfloat16 [2, 3, 1024, 512], P('section', None, 'shard'), may hold values from -0.1875 to 0.1875
- down_weight: bfloat16 [2, 3, 512, 1024], P('section', None, 'shard'), may hold values from -0.5 to 0.5
Outputs:
- section_output: float32 [2, 2, 64, 128, 1024], P('section', None, ('shard', 'replica'))
- input_gradient: float32 [2, 2, 64, 128, 1024], P('section', None, ('shard', 'replica'))
- mixer_gain_gradient: float32 [2, 1024], P('section', 'shard')
- query_weight_gradient: float32 [2, 1024, 1024], P('section', 'shard')
- key_weight_gradient: float32 [2, 1024, 512], P('section', 'shard')
- value_weight_gradient: float32 [2, 1024, 512], P('section', 'shard')
- out_weight_gradient: float32 [2, 1024, 1024], P('section', 'shard')
- expert_gain_gradient: float32 [2, 1024], P('section', 'shard')
- router_weight_gradient: float32 [2, 1024, 3], P('section', 'shard')
- gate_weight_gradient: float32 [2, 3, 1024, 512], P('section', None, 'shard')
- up_weight_gradient: float32 [2, 3, 1024, 512], P('section', None, 'shard')
- down_weight_gradient: float32 [2, 3, 512, 1024], P('section', None, 'shard')
Inputs may be any that keep to these rules, and one draw needn't show every extreme that they name: `segments`: segment numbers never fall along a packed sequence; one segment spans half of 128 tokens. `routes`: each token names 2 different experts; within one packed sequence of one micro-batch and section, no expert is named by more than 96 tokens, a bound that some block reaches.
All inputs are finite; a program needn't handle non-finite values.
Results may differ from a plain program's by a relative error of at most 0.04.
Values may be sent and summed in bfloat16 or wider, within the bound.
A program may use at most 192 MiB of HBM per device.

v0:
```python
import math

import jax
import jax.numpy as jnp
from jax import lax
from jax.sharding import PartitionSpec as P

MODEL_WIDTH = 1024
QUERY_HEADS = 16
KEY_VALUE_HEADS = 8
HEAD_SIZE = 64
E = 3
CAP = 96


epsilon = 1e-06


def passed_along(block, axis, distance):
    devices = range(lax.axis_size(axis))
    route = [(i - distance, i) for i in devices if i - distance in devices]
    return lax.ppermute(block, axis, route)


def norm_scale(hidden):
    return lax.rsqrt(jnp.mean(hidden * hidden, axis=-1, keepdims=True) + epsilon)


def rotary_tables(sequence_length, width):
    half = width // 2
    frequency = jnp.power(10000.0, -2.0 * jnp.arange(half, dtype=jnp.float32) / width)
    angles = jnp.arange(sequence_length, dtype=jnp.float32)[:, None] * frequency[None, :]
    cosine_table = jnp.concatenate([jnp.cos(angles), jnp.cos(angles)], axis=-1)[:, None, :]
    sine_table = jnp.concatenate([jnp.sin(angles), jnp.sin(angles)], axis=-1)[:, None, :]
    return (cosine_table, sine_table)


def rotate_halves(value_rows, cosine_table, sine_table):
    half = value_rows.shape[-1] // 2
    turned = jnp.concatenate([-value_rows[..., half:], value_rows[..., :half]], axis=-1)
    return value_rows * cosine_table + turned * sine_table


def norm_backward(hidden, scale, gain, incoming):
    weighted = incoming * gain.astype(jnp.float32)
    gain_part = jnp.sum(incoming * hidden * scale, axis=0)
    hidden_part = scale * weighted - hidden * (scale * scale * scale) * jnp.mean(
        weighted * hidden, axis=-1, keepdims=True
    )
    return (hidden_part, gain_part)


def route_tables(routes):
    sequence_length, picks = routes.shape
    flat = routes.reshape(sequence_length * picks)
    marks = (flat[:, None] == jnp.arange(E, dtype=jnp.int32)[None, :]).astype(jnp.int32)
    before = jnp.cumsum(marks, axis=0) - marks
    slots = jnp.sum(before * marks, axis=1).reshape(sequence_length, picks)
    target = jnp.transpose(routes * CAP + slots)
    slot_hot = (target[:, None, :] == jnp.arange(E * CAP, dtype=jnp.int32)[None, :, None]).astype(
        jnp.bfloat16
    )
    route_hot = (routes[:, :, None] == jnp.arange(E, dtype=jnp.int32)[None, None, :]).astype(
        jnp.float32
    )
    return (slot_hot, route_hot)


def layer_forward(hidden, segments, routes, weights):
    (
        mixer_gain,
        query_weight,
        key_matrix,
        value_matrix,
        out_weight,
        expert_gain,
        router_weight,
        gate_weight,
        up_weight,
        down_weight,
    ) = weights
    sequence_length = hidden.shape[0]
    repeat_factor = QUERY_HEADS // KEY_VALUE_HEADS
    cosine_table, sine_table = rotary_tables(sequence_length, HEAD_SIZE)
    scale_mixer = norm_scale(hidden)
    normalized_input = (hidden * scale_mixer * mixer_gain.astype(jnp.float32)).astype(jnp.bfloat16)
    query_rows = jnp.dot(
        normalized_input, query_weight, preferred_element_type=jnp.float32
    ).reshape(sequence_length, QUERY_HEADS, HEAD_SIZE)
    query_rows = (
        rotate_halves(query_rows, cosine_table, sine_table)
        .astype(jnp.bfloat16)
        .reshape(sequence_length, KEY_VALUE_HEADS, repeat_factor, HEAD_SIZE)
    )
    key_rows = jnp.dot(normalized_input, key_matrix, preferred_element_type=jnp.float32).reshape(
        sequence_length, KEY_VALUE_HEADS, HEAD_SIZE
    )
    key_rows = rotate_halves(key_rows, cosine_table, sine_table).astype(jnp.bfloat16)
    value_rows = (
        jnp.dot(normalized_input, value_matrix, preferred_element_type=jnp.float32)
        .astype(jnp.bfloat16)
        .reshape(sequence_length, KEY_VALUE_HEADS, HEAD_SIZE)
    )
    places = jnp.arange(sequence_length, dtype=jnp.int32)
    allowed = (segments[:, None] == segments[None, :]) & (places[None, :] <= places[:, None])
    raw = jnp.einsum("qgrd,kgd->grqk", query_rows, key_rows, preferred_element_type=jnp.float32)
    scores = jnp.where(allowed[None, None], raw * (1.0 / math.sqrt(HEAD_SIZE)), -1e30)
    top = jnp.max(scores, axis=-1, keepdims=True)
    exponent = jnp.exp(scores - top)
    total = jnp.sum(exponent, axis=-1, keepdims=True)
    attention = exponent / total
    log_total = top + jnp.log(total)
    attended = jnp.einsum(
        "grqk,kgd->qgrd",
        attention.astype(jnp.bfloat16),
        value_rows,
        preferred_element_type=jnp.float32,
    )
    attended = attended.reshape(sequence_length, QUERY_HEADS * HEAD_SIZE).astype(jnp.bfloat16)
    middle = hidden + jnp.dot(attended, out_weight, preferred_element_type=jnp.float32)
    scale_expert = norm_scale(middle)
    normed_expert = (middle * scale_expert * expert_gain.astype(jnp.float32)).astype(jnp.bfloat16)
    logits = jnp.dot(normed_expert, router_weight, preferred_element_type=jnp.float32)
    slot_hot, route_hot = route_tables(routes)
    chosen = jnp.sum(route_hot * logits[:, None, :], axis=-1)
    chosen_peak = jnp.max(chosen, axis=-1, keepdims=True)
    lifted = jnp.exp(chosen - chosen_peak)
    gates = lifted / jnp.sum(lifted, axis=-1, keepdims=True)
    dispatched = jnp.einsum(
        "kcs,sd->cd", slot_hot, normed_expert, preferred_element_type=jnp.float32
    )
    dispatched = dispatched.astype(jnp.bfloat16).reshape(E, CAP, MODEL_WIDTH)
    gate_linear = jnp.einsum(
        "ecd,edf->ecf", dispatched, gate_weight, preferred_element_type=jnp.float32
    )
    up_linear = jnp.einsum(
        "ecd,edf->ecf", dispatched, up_weight, preferred_element_type=jnp.float32
    )
    inner = (gate_linear * jax.nn.sigmoid(gate_linear) * up_linear).astype(jnp.bfloat16)
    expert_out = jnp.einsum("ecf,efd->ecd", inner, down_weight, preferred_element_type=jnp.float32)
    expert_out = expert_out.astype(jnp.bfloat16).reshape(E * CAP, MODEL_WIDTH)
    picked = jnp.einsum("kcs,cd->ksd", slot_hot, expert_out, preferred_element_type=jnp.float32)
    output = middle + jnp.sum(jnp.transpose(gates)[:, :, None] * picked, axis=0)
    kept = (
        hidden,
        scale_mixer,
        normalized_input,
        query_rows,
        key_rows,
        value_rows,
        log_total,
        attended,
        middle,
        scale_expert,
        normed_expert,
        route_hot,
        slot_hot,
        gates,
        dispatched,
        gate_linear,
        up_linear,
        inner,
        picked,
        allowed,
    )
    return (output, kept)


def layer_backward(upstream, kept, weights):
    (
        mixer_gain,
        query_weight,
        key_matrix,
        value_matrix,
        out_weight,
        expert_gain,
        router_weight,
        gate_weight,
        up_weight,
        down_weight,
    ) = weights
    (
        hidden,
        scale_mixer,
        normalized_input,
        query_rows,
        key_rows,
        value_rows,
        log_total,
        attended,
        middle,
        scale_expert,
        normed_expert,
        route_hot,
        slot_hot,
        gates,
        dispatched,
        gate_linear,
        up_linear,
        inner,
        picked,
        allowed,
    ) = kept
    sequence_length = hidden.shape[0]
    repeat_factor = QUERY_HEADS // KEY_VALUE_HEADS
    cosine_table, sine_table = rotary_tables(sequence_length, HEAD_SIZE)
    gate_columns = jnp.transpose(gates)
    back_picked = (gate_columns[:, :, None] * upstream[None]).astype(jnp.bfloat16)
    back_expert = jnp.einsum(
        "kcs,ksd->cd", slot_hot, back_picked, preferred_element_type=jnp.float32
    )
    back_expert = back_expert.astype(jnp.bfloat16).reshape(E, CAP, MODEL_WIDTH)
    down_part = jnp.einsum("ecf,ecd->efd", inner, back_expert, preferred_element_type=jnp.float32)
    back_inner = jnp.einsum(
        "ecd,efd->ecf", back_expert, down_weight, preferred_element_type=jnp.float32
    )
    sigmoid_gate = jax.nn.sigmoid(gate_linear)
    back_gate = (
        back_inner * up_linear * sigmoid_gate * (1.0 + gate_linear * (1.0 - sigmoid_gate))
    ).astype(jnp.bfloat16)
    back_up = (back_inner * gate_linear * sigmoid_gate).astype(jnp.bfloat16)
    gate_part = jnp.einsum(
        "ecd,ecf->edf", dispatched, back_gate, preferred_element_type=jnp.float32
    )
    up_part = jnp.einsum("ecd,ecf->edf", dispatched, back_up, preferred_element_type=jnp.float32)
    back_dispatched = jnp.einsum(
        "ecf,edf->ecd", back_gate, gate_weight, preferred_element_type=jnp.float32
    )
    back_dispatched = back_dispatched + jnp.einsum(
        "ecf,edf->ecd", back_up, up_weight, preferred_element_type=jnp.float32
    )
    back_dispatched = back_dispatched.astype(jnp.bfloat16).reshape(E * CAP, MODEL_WIDTH)
    back_normed_expert = jnp.einsum(
        "kcs,cd->sd", slot_hot, back_dispatched, preferred_element_type=jnp.float32
    )
    back_gates = jnp.sum(picked * upstream[None], axis=-1)
    back_chosen = gate_columns * (
        back_gates - jnp.sum(gate_columns * back_gates, axis=0, keepdims=True)
    )
    back_logits = jnp.sum(route_hot * jnp.transpose(back_chosen)[:, :, None], axis=1).astype(
        jnp.bfloat16
    )
    router_part = jnp.einsum(
        "sd,se->de", normed_expert, back_logits, preferred_element_type=jnp.float32
    )
    back_normed_expert = back_normed_expert + jnp.einsum(
        "se,de->sd", back_logits, router_weight, preferred_element_type=jnp.float32
    )
    middle_part, expert_gain_part = norm_backward(
        middle, scale_expert, expert_gain, back_normed_expert
    )
    back_middle = upstream + middle_part
    back_branch = back_middle.astype(jnp.bfloat16)
    out_part = jnp.einsum("se,sd->ed", attended, back_branch, preferred_element_type=jnp.float32)
    attended_gradient = jnp.einsum(
        "sd,ed->se", back_branch, out_weight, preferred_element_type=jnp.float32
    )
    attended_gradient = attended_gradient.astype(jnp.bfloat16).reshape(
        sequence_length, KEY_VALUE_HEADS, repeat_factor, HEAD_SIZE
    )
    raw = jnp.einsum("qgrd,kgd->grqk", query_rows, key_rows, preferred_element_type=jnp.float32)
    scores = jnp.where(allowed[None, None], raw * (1.0 / math.sqrt(HEAD_SIZE)), -1e30)
    attention = jnp.exp(scores - log_total)
    back_attention = jnp.einsum(
        "qgrd,kgd->grqk", attended_gradient, value_rows, preferred_element_type=jnp.float32
    )
    value_rows_gradient = jnp.einsum(
        "grqk,qgrd->kgd",
        attention.astype(jnp.bfloat16),
        attended_gradient,
        preferred_element_type=jnp.float32,
    )
    value_rows_gradient = value_rows_gradient.astype(jnp.bfloat16).reshape(
        sequence_length, KEY_VALUE_HEADS * HEAD_SIZE
    )
    inner_sum = jnp.sum(attention * back_attention, axis=-1, keepdims=True)
    back_scores = (attention * (back_attention - inner_sum) * (1.0 / math.sqrt(HEAD_SIZE))).astype(
        jnp.bfloat16
    )
    back_turned_queries = jnp.einsum(
        "grqk,kgd->qgrd", back_scores, key_rows, preferred_element_type=jnp.float32
    ).reshape(sequence_length, QUERY_HEADS, HEAD_SIZE)
    rotated_key_gradient = jnp.einsum(
        "grqk,qgrd->kgd", back_scores, query_rows, preferred_element_type=jnp.float32
    )
    back_queries = (
        rotate_halves(back_turned_queries, cosine_table, -sine_table)
        .astype(jnp.bfloat16)
        .reshape(sequence_length, QUERY_HEADS * HEAD_SIZE)
    )
    back_keys = (
        rotate_halves(rotated_key_gradient, cosine_table, -sine_table)
        .astype(jnp.bfloat16)
        .reshape(sequence_length, KEY_VALUE_HEADS * HEAD_SIZE)
    )
    query_part = jnp.einsum(
        "sd,se->de", normalized_input, back_queries, preferred_element_type=jnp.float32
    )
    key_part = jnp.einsum(
        "sd,se->de", normalized_input, back_keys, preferred_element_type=jnp.float32
    )
    value_part = jnp.einsum(
        "sd,se->de", normalized_input, value_rows_gradient, preferred_element_type=jnp.float32
    )
    back_normed = jnp.einsum(
        "se,de->sd", back_queries, query_weight, preferred_element_type=jnp.float32
    )
    back_normed = back_normed + jnp.einsum(
        "se,de->sd", back_keys, key_matrix, preferred_element_type=jnp.float32
    )
    back_normed = back_normed + jnp.einsum(
        "se,de->sd", value_rows_gradient, value_matrix, preferred_element_type=jnp.float32
    )
    hidden_part, mixer_gain_part = norm_backward(hidden, scale_mixer, mixer_gain, back_normed)
    back_hidden = back_middle + hidden_part
    parts = (
        mixer_gain_part,
        query_part,
        key_part,
        value_part,
        out_part,
        expert_gain_part,
        router_part,
        gate_part,
        up_part,
        down_part,
    )
    return (back_hidden, parts)


def body(
    inputs,
    cotangent,
    segments,
    routes,
    mixer_gain,
    query_weight,
    key_matrix,
    value_matrix,
    out_weight,
    expert_gain,
    router_weight,
    gate_weight,
    up_weight,
    down_weight,
):
    section_first = lax.axis_index("section") == 0
    batches = inputs.shape[0]
    local = (
        mixer_gain[0],
        query_weight[0],
        key_matrix[0],
        value_matrix[0],
        out_weight[0],
        expert_gain[0],
        router_weight[0],
        gate_weight[0],
        up_weight[0],
        down_weight[0],
    )
    token_segments = segments[:, 0]
    token_routes = routes[0, :, 0]

    def collect():
        return (
            lax.all_gather(local[0], "shard", axis=0, tiled=True),
            lax.all_gather(local[1], "shard", axis=0, tiled=True),
            lax.all_gather(local[2], "shard", axis=0, tiled=True),
            lax.all_gather(local[3], "shard", axis=0, tiled=True),
            lax.all_gather(local[4], "shard", axis=0, tiled=True),
            lax.all_gather(local[5], "shard", axis=0, tiled=True),
            lax.all_gather(local[6], "shard", axis=0, tiled=True),
            lax.all_gather(local[7], "shard", axis=1, tiled=True),
            lax.all_gather(local[8], "shard", axis=1, tiled=True),
            lax.all_gather(local[9], "shard", axis=1, tiled=True),
        )

    def pick(array, tick):
        return jnp.where(section_first, array[min(tick, batches - 1)], array[max(tick - 1, 0)])

    received = jnp.zeros(inputs.shape[2:], jnp.float32)
    tick_outputs = []
    tick_kept = []
    for tick in range(batches + 1):
        full = collect()
        own = inputs[min(tick, batches - 1), 0].astype(jnp.float32)
        hidden = jnp.where(section_first, own, received)
        output, kept = layer_forward(
            hidden, pick(token_segments, tick), pick(token_routes, tick), full
        )
        tick_outputs.append(output)
        tick_kept.append(kept)
        if tick < batches:
            received = passed_along(output.astype(jnp.bfloat16), "section", 1).astype(jnp.float32)
    returned = jnp.zeros(inputs.shape[2:], jnp.float32)
    totals = None
    tick_backs = {}
    for turn in range(batches + 1):
        tick = batches - turn
        full = collect()
        from_loss = (
            cotangent[tick - 1, 0].astype(jnp.float32)
            if tick >= 1
            else jnp.zeros(inputs.shape[2:], jnp.float32)
        )
        upstream = jnp.where(section_first, returned, from_loss)
        back_hidden, parts = layer_backward(upstream, tick_kept[tick], full)
        totals = parts if totals is None else jax.tree.map(jnp.add, totals, parts)
        tick_backs[tick] = back_hidden
        if turn < batches:
            returned = passed_along(back_hidden.astype(jnp.bfloat16), "section", -1).astype(
                jnp.float32
            )
    owned = (
        lax.psum_scatter(
            totals[0].astype(jnp.bfloat16), "shard", scatter_dimension=0, tiled=True
        ).astype(jnp.float32),
        lax.psum_scatter(
            totals[1].astype(jnp.bfloat16), "shard", scatter_dimension=0, tiled=True
        ).astype(jnp.float32),
        lax.psum_scatter(
            totals[2].astype(jnp.bfloat16), "shard", scatter_dimension=0, tiled=True
        ).astype(jnp.float32),
        lax.psum_scatter(
            totals[3].astype(jnp.bfloat16), "shard", scatter_dimension=0, tiled=True
        ).astype(jnp.float32),
        lax.psum_scatter(
            totals[4].astype(jnp.bfloat16), "shard", scatter_dimension=0, tiled=True
        ).astype(jnp.float32),
        lax.psum_scatter(
            totals[5].astype(jnp.bfloat16), "shard", scatter_dimension=0, tiled=True
        ).astype(jnp.float32),
        lax.psum_scatter(
            totals[6].astype(jnp.bfloat16), "shard", scatter_dimension=0, tiled=True
        ).astype(jnp.float32),
        lax.psum_scatter(
            totals[7].astype(jnp.bfloat16), "shard", scatter_dimension=1, tiled=True
        ).astype(jnp.float32),
        lax.psum_scatter(
            totals[8].astype(jnp.bfloat16), "shard", scatter_dimension=1, tiled=True
        ).astype(jnp.float32),
        lax.psum_scatter(
            totals[9].astype(jnp.bfloat16), "shard", scatter_dimension=1, tiled=True
        ).astype(jnp.float32),
    )
    summed = (
        lax.psum(owned[0].astype(jnp.bfloat16), "replica").astype(jnp.float32),
        lax.psum(owned[1].astype(jnp.bfloat16), "replica").astype(jnp.float32),
        lax.psum(owned[2].astype(jnp.bfloat16), "replica").astype(jnp.float32),
        lax.psum(owned[3].astype(jnp.bfloat16), "replica").astype(jnp.float32),
        lax.psum(owned[4].astype(jnp.bfloat16), "replica").astype(jnp.float32),
        lax.psum(owned[5].astype(jnp.bfloat16), "replica").astype(jnp.float32),
        lax.psum(owned[6].astype(jnp.bfloat16), "replica").astype(jnp.float32),
        lax.psum(owned[7].astype(jnp.bfloat16), "replica").astype(jnp.float32),
        lax.psum(owned[8].astype(jnp.bfloat16), "replica").astype(jnp.float32),
        lax.psum(owned[9].astype(jnp.bfloat16), "replica").astype(jnp.float32),
    )
    section_output = jnp.stack(
        [
            jnp.where(section_first, tick_outputs[index], tick_outputs[index + 1])
            for index in range(batches)
        ]
    )
    input_gradient = jnp.stack(
        [
            jnp.where(section_first, tick_backs[index], tick_backs[index + 1])
            for index in range(batches)
        ]
    )
    return (section_output[None, :, None], input_gradient[None, :, None]) + tuple(
        (piece[None] for piece in summed)
    )


def solution(mesh):
    return jax.shard_map(
        body,
        mesh=mesh,
        in_specs=(
            P(None, ("shard", "replica"), None, None),
            P(None, ("shard", "replica"), None, None),
            P(None, ("shard", "replica"), None),
            P("section", None, ("shard", "replica"), None, None),
            P("section", "shard"),
            P("section", "shard", None),
            P("section", "shard", None),
            P("section", "shard", None),
            P("section", "shard", None),
            P("section", "shard"),
            P("section", "shard", None),
            P("section", None, "shard", None),
            P("section", None, "shard", None),
            P("section", None, "shard", None),
        ),
        out_specs=(
            P("section", None, ("shard", "replica"), None, None),
            P("section", None, ("shard", "replica"), None, None),
            P("section", "shard"),
            P("section", "shard", None),
            P("section", "shard", None),
            P("section", "shard", None),
            P("section", "shard", None),
            P("section", "shard"),
            P("section", "shard", None),
            P("section", None, "shard", None),
            P("section", None, "shard", None),
            P("section", None, "shard", None),
        ),
        check_vma=False,
    )
```

profile of v0, /device:TPU:0, one launch (start us, length us, event | category | flops | bytes accessed | tf_op | source)
XLA Modules:
  0.0 777.4 jit_solution(14358604286574327134)
XLA Ops:
  27.8 10.8 %all-gather.20.cloned.1.call-done = bf16[1,1024,512]{2,1,0:T(8,128)(2,1)} async-done(((bf16[1,512,512]{2,1,0:T(8,128)(2,1)}), bf16[1,1024,512]{2,1,0:T(8,128)(2,1)}) %all-gather.20.cloned.1.call-update) | async-done | bytes 1048592 | tf_op jit(solution)/shard_map/all_gather | solution.py:368
  41.4 13.6 %all-gather.22.cloned.1.call-done = bf16[1,1024,1024]{2,1,0:T(8,128)(2,1)} async-done(((bf16[1,512,1024]{2,1,0:T(8,128)(2,1)}), bf16[1,1024,1024]{2,1,0:T(8,128)(2,1)}) %all-gather.22.cloned.1.call-update) | async-done | bytes 2097168 | tf_op jit(solution)/shard_map/all_gather | solution.py:367
  55.0 2.9 copy.172
  60.5 10.6 %all-gather.24.cloned.1.call-done = bf16[1,1024,1024]{2,1,0:T(8,128)(2,1)} async-done(((bf16[1,512,1024]{2,1,0:T(8,128)(2,1)}), bf16[1,1024,1024]{2,1,0:T(8,128)(2,1)}) %all-gather.24.cloned.1.call-update) | async-done | bytes 2097168 | tf_op jit(solution)/shard_map/all_gather | solution.py:370
  71.1 2.1 multiply_reduce_fusion.23
  74.6 14.2 %all-gather.26.cloned.1.call-done = bf16[1,3,1024,512]{3,2,1,0:T(8,128)(2,1)} async-done(((bf16[1,3,512,512]{3,2,1,0:T(8,128)(2,1)}), bf16[1,3,1024,512]{3,2,1,0:T(8,128)(2,1)}) %all-gather.26.cloned.1.call-update) | async-done | bytes 3145744 | tf_op jit(solution)/shard_map/all_gather | solution.py:373
  88.8 2.5 fusion.37
  91.4 15.1 %all-gather.28.cloned.1.call-done = bf16[1,3,1024,512]{3,2,1,0:T(8,128)(2,1)} async-done(((bf16[1,3,512,512]{3,2,1,0:T(8,128)(2,1)}), bf16[1,3,1024,512]{3,2,1,0:T(8,128)(2,1)}) %all-gather.28.cloned.1.call-update) | async-done | bytes 3145744 | tf_op jit(solution)/shard_map/all_gather | solution.py:374
  106.5 3.4 multiply_convert_fusion.11
  109.9 14.5 %all-gather.30.cloned.1.call-done = bf16[1,3,512,1024]{3,2,1,0:T(8,128)(2,1)} async-done(((bf16[1,3,256,1024]{3,2,1,0:T(8,128)(2,1)}), bf16[1,3,512,1024]{3,2,1,0:T(8,128)(2,1)}) %all-gather.30.cloned.1.call-update) | async-done | bytes 3145744 | tf_op jit(solution)/shard_map/all_gather | solution.py:375
  124.4 2.5 fusion.94
  129.3 5.3 collective-permute-start
  159.3 6.1 collective-permute-start.1
  166.0 4.3 collective-permute-done.1
  176.4 2.6 fusion.55
  187.2 3.2 fusion.7
  202.8 2.3 convolution_bitcast_fusion.5
  205.1 2.3 fusion.127
  207.4 3.6 convolution_bitcast_fusion.11
  211.0 3.7 fusion.160
  225.2 7.2 collective-permute-done.2
  242.5 2.3 convolution_bitcast_fusion.4
  244.8 2.3 fusion.128
  247.1 3.6 convolution_bitcast_fusion.9
  250.7 3.6 fusion.154
  264.7 6.5 collective-permute-done.3
  279.7 3.8 add_convert_fusion.5
  288.5 2.2 convolution_bitcast_fusion.7
  290.8 3.9 add_convert_fusion.6
  299.6 2.8 fusion.331
  302.4 2.8 fusion.332
  305.2 2.2 fusion.148
  308.5 5.7 add_convert_fusion.4
  317.7 2.7 add_convert_fusion
  323.8 2.7 add_convert_fusion.2
  329.6 2.7 add_convert_fusion.1
  334.7 7.8 %reduce-scatter.11.cloned.1.call-done = bf16[512,1024]{1,0:T(8,128)(2,1)} async-done(((bf16[1024,1024]{1,0:T(8,128)(2,1)}), bf16[512,1024]{1,0:T(8,128)(2,1)}) %reduce-scatter.11.cloned.1.call-update) | async-done | bytes 1048592 | tf_op jit(solution)/shard_map/reduce_scatter | solution.py:418
  342.5 17.8 %reduce-scatter.23.cloned.1.call-done = bf16[3,256,1024]{2,1,0:T(8,128)(2,1)} async-done(((bf16[3,512,1024]{2,1,0:T(8,128)(2,1)}), bf16[3,256,1024]{2,1,0:T(8,128)(2,1)}) %reduce-scatter.23.cloned.1.call-update) | async-done | bytes 1572880 | tf_op jit(solution)/shard_map/reduce_scatter | solution.py:442
  360.3 18.0 %reduce-scatter.19.cloned.1.call-done = bf16[3,512,512]{2,1,0:T(8,128)(2,1)} async-done(((bf16[3,1024,512]{2,1,0:T(8,128)(2,1)}), bf16[3,512,512]{2,1,0:T(8,128)(2,1)}) %reduce-scatter.19.cloned.1.call-update) | async-done | bytes 1572880 | tf_op jit(solution)/shard_map/reduce_scatter | solution.py:436
  378.3 17.7 %reduce-scatter.21.cloned.1.call-done = bf16[3,512,512]{2,1,0:T(8,128)(2,1)} async-done(((bf16[3,1024,512]{2,1,0:T(8,128)(2,1)}), bf16[3,512,512]{2,1,0:T(8,128)(2,1)}) %reduce-scatter.21.cloned.1.call-update) | async-done | bytes 1572880 | tf_op jit(solution)/shard_map/reduce_scatter | solution.py:439
  398.0 2.4 maximum_bitcast_fusion
  403.7 2.5 all-reduce.4
  407.7 2.3 reduce-scatter.25.cloned.1.call-done
  411.0 84.6 %all-reduce.2 = (bf16[1,512]{1,0:T(2,128)(2,1)S(1)}, bf16[1,512]{1,0:T(2,128)(2,1)S(1)}, bf16[1,512,3]{1,2,0:T(4,128)(2,1)S(1)}) all-reduce(bf16[1,512]{1,0:T(2,128)(2,1)S(1)} %broadcast_in_dim.96, bf16[1,512]{1,0:T(2,128)(2,1)S(1)} %broadcast_in_dim.106, ...), channel_id=1, replica_groups=mesh['section'=2,'shard'=2,'replica'=32] {'replica'}, use_global_device_ids=true, to_apply=%region_58.59 | all-reduce | flops 2560 | bytes 10240 | tf_op jit(solution)/shard_map/psum | solution.py:447
  497.3 260.4 %all-reduce.7.cloned.1.call-done = (bf16[1,512,1024]{2,1,0:T(8,128)(2,1)}, bf16[1,512,512]{2,1,0:T(8,128)(2,1)}, bf16[1,512,512]{2,1,0:T(8,128)(2,1)}, bf16[1,51...) async-done(((bf16[1,512,1024]{2,1,0:T(8,128)(2,1)}, ...) | async-done | bytes 7864336 | tf_op jit(solution)/shard_map/psum | solution.py:448
  757.7 2.9 broadcast_in_dim.99
  764.4 2.1 broadcast_in_dim.111
  766.5 2.1 broadcast_in_dim.113
  (704 shorter events, 156.1 us)
Async XLA Ops:
  7.2 18.3 %all-gather.18.cloned.1.call-start = ((), (), s32[]{:S(2)}) async-start(), calls=%async_computation.15 | async-start | bytes 1572864 | tf_op jit(solution)/shard_map/all_gather | solution.py:369
  7.9 30.7 %all-gather.20.cloned.1.call-start = ((), (), s32[]{:S(2)}) async-start(), calls=%async_computation.16 | async-start | bytes 1572864 | tf_op jit(solution)/shard_map/all_gather | solution.py:368
  8.7 46.3 %all-gather.22.cloned.1.call-start = ((), (), s32[]{:S(2)}) async-start(), calls=%async_computation.17 | async-start | bytes 3145728 | tf_op jit(solution)/shard_map/all_gather | solution.py:367
  9.5 61.7 %all-gather.24.cloned.1.call-start = ((), (), s32[]{:S(2)}) async-start(), calls=%async_computation.18 | async-start | bytes 3145728 | tf_op jit(solution)/shard_map/all_gather | solution.py:370
  10.0 78.8 %all-gather.26.cloned.1.call-start = ((), (), s32[]{:S(2)}) async-start(), calls=%async_computation.19 | async-start | bytes 4718592 | tf_op jit(solution)/shard_map/all_gather | solution.py:373
  10.6 95.9 %all-gather.28.cloned.1.call-start = ((), (), s32[]{:S(2)}) async-start(), calls=%async_computation.20 | async-start | bytes 4718592 | tf_op jit(solution)/shard_map/all_gather | solution.py:374
  11.2 113.2 %all-gather.30.cloned.1.call-start = ((), (), s32[]{:S(2)}) async-start(), calls=%async_computation.21 | async-start | bytes 4718592 | tf_op jit(solution)/shard_map/all_gather | solution.py:375
  11.9 322.7 %reduce-scatter.15.cloned.1.call-start = ((), (), s32[]{:S(2)}) async-start(), calls=%async_computation.10 | async-start | bytes 1572864 | tf_op jit(solution)/shard_map/reduce_scatter | solution.py:424
  13.7 44.2 %copy-start.159 = (f32[128]{0:T(128)}, f32[128]{0:T(128)S(1)}, u32[]{:S(2)}) copy-start(f32[128]{0:T(128)S(1)} %get-tuple-element.142) | copy-start | bytes 1540
  20.8 53.3 %copy-start.173 = (s32[128,2]{0,1:T(2,128)}, s32[128,2]{0,1:T(2,128)S(1)}, u32[]{:S(2)}) copy-start(s32[128,2]{0,1:T(2,128)S(1)} %copy.175) | copy-start | bytes 3076
  23.9 110.7 %copy-start.163 = (s32[2,128]{1,0:T(2,128)}, s32[2,128]{1,0:T(2,128)S(1)}, u32[]{:S(2)}) copy-start(s32[2,128]{1,0:T(2,128)S(1)} %copy.188) | copy-start | bytes 3076
  24.0 16.7 %copy-start.178 = (s32[2,128]{1,0:T(2,128)}, s32[2,128]{1,0:T(2,128)S(1)}, u32[]{:S(2)}) copy-start(s32[2,128]{1,0:T(2,128)S(1)} %copy.197) | copy-start | bytes 3076
  24.1 102.8 %copy-start.161 = (s32[2,128]{1,0:T(2,128)}, s32[2,128]{1,0:T(2,128)S(1)}, u32[]{:S(2)}) copy-start(s32[2,128]{1,0:T(2,128)S(1)} %copy.178) | copy-start | bytes 3076
  24.2 50.1 %copy-start.137 = (bf16[288,128]{1,0:T(8,128)(2,1)}, bf16[288,128]{1,0:T(8,128)(2,1)S(1)}, u32[]{:S(2)}) copy-start(bf16[288,128]{1,0:T(8,128)(2,1)S(1)} %convert_reduce_fusion.2) | copy-start | bytes 221188
  59.4 13.9 %copy-start.155 = (f32[8,2,128]{2,1,0:T(2,128)}, f32[8,2,128]{2,1,0:T(2,128)S(1)}, u32[]{:S(2)}) copy-start(f32[8,2,128]{2,1,0:T(2,128)S(1)} %fusion.162) | copy-start | bytes 24580
  60.5 13.8 %copy-start.122 = (bf16[8,64,2,128]{3,1,2,0:T(8,128)(2,1)}, bf16[8,64,2,128]{3,1,2,0:T(8,128)(2,1)S(1)}, u32[]{:S(2)}) copy-start(bf16[8,64,2,128]{3,1,2,0:T(8,128)(2,1)S(1)} %convolution_convert_fusion.5) | copy-start | bytes 786436
  73.3 55.2 %copy-start.32 = (f32[128,1024]{1,0:T(8,128)}, f32[128,1024]{1,0:T(8,128)S(1)}, u32[]{:S(2)}) copy-start(f32[128,1024]{1,0:T(8,128)S(1)} %get-tuple-element.158) | copy-start | bytes 1572868
  73.9 17.5 %copy-start.184 = (f32[128]{0:T(128)}, f32[128]{0:T(128)S(1)}, u32[]{:S(2)}) copy-start(f32[128]{0:T(128)S(1)} %get-tuple-element.144) | copy-start | bytes 1540
  74.0 17.4 %copy-start.71 = (bf16[128,1024]{1,0:T(8,128)(2,1)}, bf16[128,1024]{1,0:T(8,128)(2,1)S(1)}, u32[]{:S(2)}) copy-start(bf16[128,1024]{1,0:T(8,128)(2,1)S(1)} %multiply_convert_fusion.19) | copy-start | bytes 786436
  74.2 17.2 %copy-start.152 = (f32[128,2]{0,1:T(2,128)}, f32[128,2]{0,1:T(2,128)S(1)}, u32[]{:S(2)}) copy-start(f32[128,2]{0,1:T(2,128)S(1)} %select_reduce_fusion.5) | copy-start | bytes 3076
  74.2 17.1 %copy-start.165 = (f32[128]{0:T(128)}, f32[128]{0:T(128)S(1)}, u32[]{:S(2)}) copy-start(f32[128]{0:T(128)S(1)} %reduce_max.55) | copy-start | bytes 1540
  74.3 17.1 %copy-start.180 = (f32[128]{0:T(128)}, f32[128]{0:T(128)S(1)}, u32[]{:S(2)}) copy-start(f32[128]{0:T(128)S(1)} %fusion.303) | copy-start | bytes 1540
  74.3 52.6 %copy-start.169 = (f32[2,128]{1,0:T(2,128)}, f32[2,128]{1,0:T(2,128)S(1)}, u32[]{:S(2)}) copy-start(f32[2,128]{1,0:T(2,128)S(1)} %fusion.474) | copy-start | bytes 3076
  74.6 35.3 %copy-start.40 = (bf16[288,1024]{1,0:T(8,128)(2,1)}, bf16[288,1024]{1,0:T(8,128)(2,1)S(1)}, u32[]{:S(2)}) copy-start(bf16[288,1024]{1,0:T(8,128)(2,1)S(1)} %fusion.345) | copy-start | bytes 1769476
  91.4 18.5 %copy-start.133 = (f32[3,96,512]{2,1,0:T(8,128)}, f32[3,96,512]{2,1,0:T(8,128)S(1)}, u32[]{:S(2)}) copy-start(f32[3,96,512]{2,1,0:T(8,128)S(1)} %fusion.37) | copy-start | bytes 1769476
  109.9 17.0 %copy-start.119 = (bf16[3,96,512]{2,1,0:T(8,128)(2,1)}, bf16[3,96,512]{2,1,0:T(8,128)(2,1)S(1)}, u32[]{:S(2)}) copy-start(bf16[3,96,512]{2,1,0:T(8,128)(2,1)S(1)} %get-tuple-element.159) | copy-start | bytes 884740
  129.3 15.5 %copy-start.1 = (bf16[1,1024,1024]{2,1,0:T(8,128)(2,1)S(1)}, bf16[1,1024,1024]{2,1,0:T(8,128)(2,1)}, u32[]{:S(2)}) copy-start(bf16[1,1024,1024]{2,1,0:T(8,128)(2,1)} %all-gather.22.cloned.1.call-done) | copy-start | bytes 6291460
  129.3 11.2 %collective-permute-start = (bf16[128,1024]{1,0:T(8,128)(2,1)S(1)}, bf16[128,1024]{1,0:T(8,128)(2,1)S(1)}, u32[]{:S(2)}, u32[]{:S(2)}) collective-permute-start(bf16[128,1024]{1,0:T(8,128)(2,1)S(1)} %get-tuple-element.94), channel_id=1, source_target_pairs={{0,64},{1,65},{2,66},{3,67},{4,68},{5,69},{6,70},{7,71},{8,72},{9,... | collective-permute-start | bytes 786440 | tf_op jit(solution)/shard_map/ppermute | solution.py:22
  156.7 13.6 %copy-start.20 = (bf16[2,1,128,1024]{3,2,1,0:T(8,128)(2,1)S(1)}, bf16[2,1,128,1024]{3,2,1,0:T(8,128)(2,1)}, u32[]{:S(2)}) copy-start(bf16[2,1,128,1024]{3,2,1,0:T(8,128)(2,1)} %param.14) | copy-start | bytes 1572868
  156.8 15.2 %copy-start.28 = (bf16[1,1024,512]{2,1,0:T(8,128)(2,1)S(1)}, bf16[1,1024,512]{2,1,0:T(8,128)(2,1)}, u32[]{:S(2)}) copy-start(bf16[1,1024,512]{2,1,0:T(8,128)(2,1)} %all-gather.18.cloned.1.call-done) | copy-start | bytes 3145732
  159.2 12.0 %copy-start.66 = (f32[128,1024]{1,0:T(8,128)}, f32[128,1024]{1,0:T(8,128)S(1)}, u32[]{:S(2)}) copy-start(f32[128,1024]{1,0:T(8,128)S(1)} %get-tuple-element.91) | copy-start | bytes 1572868
  159.3 11.1 %collective-permute-start.1 = (bf16[128,1024]{1,0:T(8,128)(2,1)S(1)}, bf16[128,1024]{1,0:T(8,128)(2,1)S(1)}, u32[]{:S(2)}, u32[]{:S(2)}) collective-permute-start(bf16[128,1024]{1,0:T(8,128)(2,1)S(1)} %convert_element_type.469), channel_id=1, source_target_pairs={{0,64},{1,65},{2,66},{3,67},{4,68},{5,69},{6,70},{7,71},{8,72},{9,... | collective-permute-start | bytes 786440 | tf_op jit(solution)/shard_map/ppermute | solution.py:22
  220.1 12.3 %copy-start.110 = (bf16[2,1,128,1024]{3,2,1,0:T(8,128)(2,1)S(1)}, bf16[2,1,128,1024]{3,2,1,0:T(8,128)(2,1)}, u32[]{:S(2)}) copy-start(bf16[2,1,128,1024]{3,2,1,0:T(8,128)(2,1)} %param.15) | copy-start | bytes 1572868
  220.7 11.8 %copy-start.172 = (f32[2,128]{1,0:T(2,128)S(1)}, f32[2,128]{1,0:T(2,128)}, u32[]{:S(2)}) copy-start(f32[2,128]{1,0:T(2,128)} %copy-done.171) | copy-start | bytes 3076
  220.8 12.2 %copy-start.70 = (f32[2,128,1024]{2,1,0:T(8,128)S(1)}, f32[2,128,1024]{2,1,0:T(8,128)}, u32[]{:S(2)}) copy-start(f32[2,128,1024]{2,1,0:T(8,128)} %get-tuple-element.170) | copy-start | bytes 3145732
  221.8 11.4 %copy-start.136 = (f32[3,96,512]{2,1,0:T(8,128)S(1)}, f32[3,96,512]{2,1,0:T(8,128)}, u32[]{:S(2)}) copy-start(f32[3,96,512]{2,1,0:T(8,128)} %copy-done.135) | copy-start | bytes 1769476
  221.8 11.4 %copy-start.205 = (f32[3,96,512]{2,1,0:T(8,128)S(1)}, f32[3,96,512]{2,1,0:T(8,128)}, u32[]{:S(2)}) copy-start(f32[3,96,512]{2,1,0:T(8,128)} %get-tuple-element.168) | copy-start | bytes 1769476
  221.9 10.6 %collective-permute-start.2 = (bf16[128,1024]{1,0:T(8,128)(2,1)S(1)}, bf16[128,1024]{1,0:T(8,128)(2,1)S(1)}, u32[]{:S(2)}, u32[]{:S(2)}) collective-permute-start(bf16[128,1024]{1,0:T(8,128)(2,1)S(1)} %get-tuple-element.88), channel_id=1, source_target_pairs={{64,0},{65,1},{66,2},{67,3},{68,4},{69,5},{70,6},{71,7},{72,8},{73... | collective-permute-start | bytes 786440 | tf_op jit(solution)/shard_map/ppermute | solution.py:22
  260.1 11.6 %copy-start.69 = (f32[2,128,1024]{2,1,0:T(8,128)S(1)}, f32[2,128,1024]{2,1,0:T(8,128)}, u32[]{:S(2)}) copy-start(f32[2,128,1024]{2,1,0:T(8,128)} %get-tuple-element.162) | copy-start | bytes 3145732
  261.2 10.0 %collective-permute-start.3 = (bf16[128,1024]{1,0:T(8,128)(2,1)S(1)}, bf16[128,1024]{1,0:T(8,128)(2,1)S(1)}, u32[]{:S(2)}, u32[]{:S(2)}) collective-permute-start(bf16[128,1024]{1,0:T(8,128)(2,1)S(1)} %get-tuple-element.86), channel_id=1, source_target_pairs={{64,0},{65,1},{66,2},{67,3},{68,4},{69,5},{70,6},{71,7},{72,8},{73... | collective-permute-start | bytes 786440 | tf_op jit(solution)/shard_map/ppermute | solution.py:22
  283.6 51.2 %reduce-scatter.13.cloned.1.call-start = ((), (), s32[]{:S(2)}) async-start(), calls=%async_computation.9 | async-start | bytes 1572864 | tf_op jit(solution)/shard_map/reduce_scatter | solution.py:421
  294.8 40.0 %reduce-scatter.17.cloned.1.call-start = ((), (), s32[]{:S(2)}) async-start(), calls=%async_computation.11 | async-start | bytes 3145728 | tf_op jit(solution)/shard_map/reduce_scatter | solution.py:427
  299.6 42.9 %reduce-scatter.11.cloned.1.call-start = ((), (), s32[]{:S(2)}) async-start(), calls=%async_computation.8 | async-start | bytes 3145728 | tf_op jit(solution)/shard_map/reduce_scatter | solution.py:418
  314.2 46.1 %reduce-scatter.23.cloned.1.call-start = ((), (), s32[]{:S(2)}) async-start(), calls=%async_computation.14 | async-start | bytes 4718592 | tf_op jit(solution)/shard_map/reduce_scatter | solution.py:442
  320.4 57.9 %reduce-scatter.19.cloned.1.call-start = ((), (), s32[]{:S(2)}) async-start(), calls=%async_computation.12 | async-start | bytes 4718592 | tf_op jit(solution)/shard_map/reduce_scatter | solution.py:436
  326.5 69.5 %reduce-scatter.21.cloned.1.call-start = ((), (), s32[]{:S(2)}) async-start(), calls=%async_computation.13 | async-start | bytes 4718592 | tf_op jit(solution)/shard_map/reduce_scatter | solution.py:439
  332.3 77.7 %reduce-scatter.25.cloned.1.call-start = ((), (), s32[]{:S(2)}) async-start(), calls=%async_computation.22 | async-start | bytes 393216
  334.6 423.0 %all-reduce.7.cloned.1.call-start = ((), (), s32[]{:S(2)}) async-start(), calls=%async_computation.23 | async-start | bytes 15728640 | tf_op jit(solution)/shard_map/psum | solution.py:448
  (178 other events, 571.4 us)
Sparse Core Ops, SparseCore 0:
  9.7 14.1 all-gather.17
  25.5 13.0 all-gather.19
  40.3 14.6 all-gather.21
  56.5 14.6 all-gather.23
  72.6 16.1 all-gather.25
  90.3 16.1 all-gather.27
  108.2 16.1 all-gather.29
  283.7 9.9 reduce-scatter.14
  296.7 12.5 reduce-scatter.12
  312.0 13.6 reduce-scatter.16
  328.8 13.6 reduce-scatter.10
  345.3 14.9 reduce-scatter.22
  363.3 14.9 reduce-scatter.18
  381.1 14.9 reduce-scatter.20
  398.3 11.6 reduce-scatter.24
  412.9 344.6 all-reduce.6
where the time goes:
time: 785 us; the launch traced here: 777 us
  waiting for transfers between devices  427 us (54%)
  matrix products  141 us (18%)
  blocking collectives  92.4 us (12%)
  other arithmetic  47.7 us (6%)
  local copies, waits for them, and re-layouts  35 us (4%)
  between operations  18 us (2%)
  starting transfers between devices  15.6 us (2%)
    psum x1, waiting for transfers between devices, body(): lax.psum(owned[1].astype(jnp.bfloat16), 'replica').astype(jnp.float32)  260 us
    psum x1, blocking collectives, body(): lax.psum(owned[0].astype(jnp.bfloat16), 'replica').astype(jnp.float32)  84.6 us
    unnamed x420, local copies, waits for them, and re-layouts  21 us
    ppermute x4, waiting for transfers between devices, passed_along(): return lax.ppermute(block, axis, route)  20.1 us
    reduce_scatter x1, waiting for transfers between devices, body(): lax.psum_scatter(totals[7].astype(jnp.bfloat16), 'shard', scatter_dimensi...  18 us
    reduce_scatter x1, waiting for transfers between devices, body(): lax.psum_scatter(totals[9].astype(jnp.bfloat16), 'shard', scatter_dimensi...  17.8 us
    reduce_scatter x1, waiting for transfers between devices, body(): lax.psum_scatter(totals[8].astype(jnp.bfloat16), 'shard', scatter_dimensi...  17.7 us
  transfers between devices with their start and end apart: 20, of which 16 were waited for; matrix products, arithmetic and copies ran while one was open for 12% of the time, Pallas kernels for 0%

commit v1 on v0

v1 whole, which is shorter than its diff:
```python
import functools

import numpy as np
import jax
import jax.numpy as jnp
from jax import lax
from jax.experimental import pallas as pl
from jax.experimental.pallas import tpu as pltpu
from jax.sharding import PartitionSpec as P

MESH = pl.DeviceIdType.MESH
ROWS = 7680
COLS = 512
PARTS = 5
PART = ROWS // PARTS
DIMS = 5


def cube_position():
    r = lax.axis_index("replica")
    x = r % 4
    z = (r // 4) % 4
    y = r // 16
    bits = (((x + 1) // 2) % 2, x // 2, ((z + 1) // 2) % 2, z // 2, y)
    partners = (
        r + 1 - 2 * (x % 2),
        r + 3 - 2 * x,
        r + 4 - 8 * (z % 2),
        r + 12 - 8 * z,
        (r + 16) % 32,
    )
    return bits, partners


def add_rows(dst, dst_at, a, a_at, b, b_at, count):
    step = min(count, 192)

    def one(i, carry):
        at = i * step
        dst[pl.ds(pl.multiple_of(dst_at + at, 16), step), :] = (
            a[pl.ds(pl.multiple_of(a_at + at, 16), step), :]
            + b[pl.ds(pl.multiple_of(b_at + at, 16), step), :]
        )
        return carry

    lax.fori_loop(0, count // step, one, 0)


def reduce_kernel(
    parts_ref, small_ref, out_ref, small_out,
    work, from_core, from_cube, whole, small_held, small_got,
    load_sem, core_send, core_recv, cube_send, cube_recv,
    share_send, share_recv, small_send, small_recv, store_sem,
):
    core = lax.axis_index("shard")
    bits, partners = cube_position()
    sibling = {"shard": 1 - core}

    barrier = pltpu.get_barrier_semaphore()
    pl.semaphore_signal(barrier, inc=1, device_id=sibling, device_id_type=MESH)
    for partner in partners:
        pl.semaphore_signal(barrier, inc=1, device_id={"replica": partner}, device_id_type=MESH)

    loads = []
    for p in range(PARTS):
        load = pltpu.make_async_copy(
            parts_ref.at[core, pl.ds(p * PART, PART)], work.at[pl.ds(p * PART, PART)], load_sem.at[p]
        )
        load.start()
        loads.append(load)
    pl.semaphore_wait(barrier, 1 + DIMS)

    cores = []
    small_core = pltpu.make_async_remote_copy(
        src_ref=small_ref.at[1 - core], dst_ref=small_got.at[0],
        send_sem=small_send.at[0], recv_sem=small_recv.at[0],
        device_id=sibling, device_id_type=MESH,
    )
    small_core.start()
    for p in range(PARTS):
        copy = pltpu.make_async_remote_copy(
            src_ref=parts_ref.at[1 - core, pl.ds(p * PART, PART)],
            dst_ref=from_core.at[pl.ds(p * PART, PART)],
            send_sem=core_send.at[p], recv_sem=core_recv.at[p],
            device_id=sibling, device_id_type=MESH,
        )
        copy.start()
        cores.append(copy)

    sends = [small_core] + cores
    kept = [0] * PARTS

    def start_scatter(p, s):
        d = (p + s) % DIMS
        size = PART >> (s + 1)
        slot = p * PART + PART - (PART >> s)
        away = kept[p] + (1 - bits[d]) * size
        kept[p] = kept[p] + bits[d] * size
        copy = pltpu.make_async_remote_copy(
            src_ref=work.at[pl.ds(pl.multiple_of(p * PART + away, 16), size)],
            dst_ref=from_cube.at[pl.ds(slot, size)],
            send_sem=cube_send.at[p * DIMS + s], recv_sem=cube_recv.at[p * DIMS + s],
            device_id={"replica": partners[d]}, device_id_type=MESH,
        )
        copy.start()
        sends.append(copy)
        return copy

    def start_small(s):
        copy = pltpu.make_async_remote_copy(
            src_ref=small_held.at[s], dst_ref=small_got.at[s + 1],
            send_sem=small_send.at[s + 1], recv_sem=small_recv.at[s + 1],
            device_id={"replica": partners[s]}, device_id_type=MESH,
        )
        copy.start()
        sends.append(copy)
        return copy

    def start_share(p, s):
        d = (p + s) % DIMS
        size = PART >> (s + 1)
        copy = pltpu.make_async_remote_copy(
            src_ref=whole.at[pl.ds(pl.multiple_of(p * PART + kept[p], 16), size)],
            dst_ref=whole.at[pl.ds(pl.multiple_of(p * PART + kept[p], 16), size)],
            send_sem=share_send.at[p * DIMS + s], recv_sem=share_recv.at[p * DIMS + s],
            device_id={"replica": partners[d]}, device_id_type=MESH,
        )
        copy.start()
        sends.append(copy)
        return copy

    stores = []

    def start_store(at, size, index):
        copy = pltpu.make_async_copy(
            whole.at[pl.ds(pl.multiple_of(at, 16), size)],
            out_ref.at[pl.ds(pl.multiple_of(at, 16), size)],
            store_sem.at[index],
        )
        copy.start()
        stores.append(copy)

    cube = [None] * PARTS
    for p in range(PARTS):
        loads[p].wait()
        cores[p].wait_recv()
        add_rows(work, p * PART, work, p * PART, from_core, p * PART, PART)
        cube[p] = start_scatter(p, 0)
    small_core.wait_recv()
    small_held[0] = small_ref[core] + small_got[0]
    small = start_small(0)

    share = [None] * PARTS
    for s in range(DIMS):
        for p in range(PARTS):
            cube[p].wait_recv()
            size = PART >> (s + 1)
            slot = p * PART + PART - (PART >> s)
            at = p * PART + kept[p]
            last = s == DIMS - 1
            add_rows(whole if last else work, at, work, at, from_cube, slot, size)
            if last:
                share[p] = start_share(p, s)
                start_store(at, size, p)
            else:
                cube[p] = start_scatter(p, s + 1)
        small.wait_recv()
        if s < DIMS - 1:
            small_held[s + 1] = small_held[s] + small_got[s + 1]
            small = start_small(s + 1)
        else:
            small_out[...] = small_held[s] + small_got[s + 1]

    for s in reversed(range(DIMS)):
        for p in range(PARTS):
            d = (p + s) % DIMS
            size = PART >> (s + 1)
            share[p].wait_recv()
            got = kept[p] + size - 2 * bits[d] * size
            kept[p] = kept[p] - bits[d] * size
            if s > 0:
                share[p] = start_share(p, s - 1)
            start_store(p * PART + got, size, PARTS + p * DIMS + s)

    for copy in sends:
        copy.wait_send()
    for copy in stores:
        copy.wait()


def reduce_gradients(parts, small):
    dma = pltpu.SemaphoreType.DMA
    return pl.pallas_call(
        reduce_kernel,
        out_shape=(
            jax.ShapeDtypeStruct((ROWS, COLS), jnp.bfloat16),
            jax.ShapeDtypeStruct((16, COLS), jnp.float32),
        ),
        in_specs=[pl.BlockSpec(memory_space=pl.ANY), pl.BlockSpec(memory_space=pltpu.VMEM)],
        out_specs=(pl.BlockSpec(memory_space=pl.ANY), pl.BlockSpec(memory_space=pltpu.VMEM)),
        scratch_shapes=[
            pltpu.VMEM((ROWS, COLS), jnp.bfloat16),
            pltpu.VMEM((ROWS, COLS), jnp.bfloat16),
            pltpu.VMEM((ROWS, COLS), jnp.bfloat16),
            pltpu.VMEM((ROWS, COLS), jnp.bfloat16),
            pltpu.VMEM((DIMS, 16, COLS), jnp.float32),
            pltpu.VMEM((DIMS + 1, 16, COLS), jnp.float32),
            dma((PARTS,)), dma((PARTS,)), dma((PARTS,)),
            dma((PARTS * DIMS,)), dma((PARTS * DIMS,)),
            dma((PARTS * DIMS,)), dma((PARTS * DIMS,)),
            dma((DIMS + 1,)), dma((DIMS + 1,)),
            dma((PARTS + PARTS * DIMS,)),
        ],
        compiler_params=pltpu.CompilerParams(
            collective_id=1, has_side_effects=True, vmem_limit_bytes=48 * 1024 * 1024
        ),
    )(parts, small)


def gather_kernel(count, *refs):
    mine, others = refs[:count], refs[count:2 * count]
    send_sem, recv_sem = refs[2 * count:]
    sibling = {"shard": 1 - lax.axis_index("shard")}
    barrier = pltpu.get_barrier_semaphore()
    pl.semaphore_signal(barrier, inc=1, device_id=sibling, device_id_type=MESH)
    pl.semaphore_wait(barrier, 1)
    copies = []
    for i in range(count):
        copy = pltpu.make_async_remote_copy(
            src_ref=mine[i], dst_ref=others[i],
            send_sem=send_sem.at[i], recv_sem=recv_sem.at[i],
            device_id=sibling, device_id_type=MESH,
        )
        copy.start()
        copies.append(copy)
    for copy in copies:
        copy.wait()


def exchange(*arrays):
    n = len(arrays)
    return pl.pallas_call(
        functools.partial(gather_kernel, n),
        out_shape=tuple(jax.ShapeDtypeStruct(a.shape, a.dtype) for a in arrays),
        in_specs=[pl.BlockSpec(memory_space=pl.ANY)] * n,
        out_specs=tuple(pl.BlockSpec(memory_space=pl.ANY) for _ in arrays),
        scratch_shapes=[pltpu.SemaphoreType.DMA((n,)), pltpu.SemaphoreType.DMA((n,))],
        compiler_params=pltpu.CompilerParams(collective_id=2, has_side_effects=True),
    )(*arrays)


EPSILON = 1e-06
WEIGHT_SHAPES = (
    (1024, 1024), (1024, 512), (1024, 512), (1024, 1024), (3, 1024, 512), (3, 1024, 512), (3, 512, 1024),
)
NT = (((1,), (1,)), ((), ()))
NN = (((1,), (0,)), ((), ()))
TN = (((0,), (0,)), ((), ()))
F32 = jnp.float32
BF16 = jnp.bfloat16
TOKENS = 256
WIDTH = 1024
VMEM_LIMIT = 56 * 1024 * 1024


def dot(a, b, dims):
    return lax.dot_general(a, b, dims, preferred_element_type=F32)


def weight_copies(mine, others, held, sems):
    core = lax.axis_index("shard")
    copies = []
    for i, (a, b, w) in enumerate(zip(mine, others, held)):
        rows = a.shape[-2]
        axis = len(a.shape) - 2
        pair = []
        for j, (source, owner) in enumerate(((a, core), (b, 1 - core))):
            place = pl.ds(pl.multiple_of(owner * rows, rows), rows)
            target = w.at[place] if axis == 0 else w.at[:, place]
            pair.append(pltpu.make_async_copy(source, target, sems.at[2 * i + j]))
        copies.append(pair)
    return copies


def start_all(copies, order):
    for i in order:
        for copy in copies[i]:
            copy.start()


def arrive(copies, *which):
    for i in which:
        for copy in copies[i]:
            copy.wait()


def small_rows(mine, other):
    first = lax.axis_index("shard") == 0
    a, b = mine[...], other[...]
    return jnp.concatenate([jnp.where(first, a, b), jnp.where(first, b, a)], axis=1)


def scale_of(rows):
    return lax.rsqrt(jnp.mean(rows * rows, axis=-1, keepdims=True) + EPSILON)


def swap_halves(u):
    lanes = u.shape[1]
    lane = lax.broadcasted_iota(jnp.int32, u.shape, 1)
    return jnp.where(lane % 64 < 32, pltpu.roll(u, lanes - 32, 1), pltpu.roll(u, 32, 1))


def low_half(shape):
    return lax.broadcasted_iota(jnp.int32, shape, 1) < 64


def both_ways(block):
    wide = block.astype(F32)
    turned = pltpu.roll(wide, 64, 1)
    low = low_half(wide.shape)
    return jnp.where(low, wide, turned).astype(BF16), jnp.where(low, turned, wide).astype(BF16)


def stack_heads(block):
    wide = block.astype(F32)
    low = low_half(wide.shape)
    zero = jnp.zeros_like(wide)
    return jnp.concatenate([jnp.where(low, wide, zero), jnp.where(low, zero, wide)], axis=0).astype(BF16)


def join_heads(rows):
    return jnp.where(low_half((128, 128)), rows[:128], rows[128:])


def forward_kernel(
    start_ref, received_ref, bias_ref, marks_ref, cos_ref, sin_ref, small_mine, small_other, *refs
):
    mine, others, refs = refs[:7], refs[7:14], refs[14:]
    (relay_ref, out_ref, hidden_ref, normed_ref, q_ref, k_ref, v_ref, p_ref, att_ref, middle_ref, ne_ref,
     gates_ref, gl_ref, ul_ref, gi_ref) = refs[:15]
    held, sems = refs[15:22], refs[22]
    wq, wk, wv, wo, wg, wu, wd = held
    copies = weight_copies(mine, others, held, sems)
    start_all(copies, range(7))
    small = small_rows(small_mine, small_other)
    first = lax.axis_index("section") == 0
    hidden = jnp.where(first, start_ref[...], received_ref[...])
    hidden_ref[...] = hidden
    x = hidden.astype(F32)
    normed_ref[...] = (x * scale_of(x) * small[0:1].astype(F32)).astype(BF16)

    def block(ref, i, size=256):
        return ref[:, i * size:(i + 1) * size]

    for weight, target, number, turned, index in (
        (wq, q_ref, 4, True, 0), (wk, k_ref, 2, True, 1), (wv, v_ref, 2, False, 2),
    ):
        arrive(copies, index)
        for i in range(number):
            u = dot(normed_ref[...], block(weight, i), NN)
            if turned:
                u = u * cos_ref[...] + swap_halves(u) * sin_ref[...]
            target[:, i * 256:(i + 1) * 256] = u.astype(BF16)

    for pack in range(2):
        rows = slice(pack * 128, pack * 128 + 128)
        bias = bias_ref[pack]
        bias = jnp.concatenate([bias, bias], axis=0)
        for pair in range(4):
            keys = both_ways(k_ref[rows, pair * 128:(pair + 1) * 128])
            values = both_ways(v_ref[rows, pair * 128:(pair + 1) * 128])
            for half in range(2):
                g = pair * 2 + half
                queries = stack_heads(q_ref[rows, g * 128:(g + 1) * 128])
                scores = dot(queries, keys[half], NT) * 0.125 + bias
                exponent = jnp.exp(scores - jnp.max(scores, axis=-1, keepdims=True))
                attention = (exponent / jnp.sum(exponent, axis=-1, keepdims=True)).astype(BF16)
                p_ref[pack, g] = attention
                att_ref[rows, g * 128:(g + 1) * 128] = join_heads(dot(attention, values[half], NN)).astype(BF16)

    arrive(copies, 3)
    for i in range(4):
        cols = slice(i * 256, (i + 1) * 256)
        middle_ref[:, cols] = hidden_ref[:, cols].astype(F32) + dot(att_ref[...], wo[:, cols], NN)
    middle = middle_ref[...]
    ne_ref[...] = (middle * scale_of(middle) * small[1:2].astype(F32)).astype(BF16)
    logits = dot(ne_ref[...], small, NT)
    marks = marks_ref[...] > 0.0
    peak = jnp.max(jnp.where(marks, logits, -1e30), axis=-1, keepdims=True)
    lifted = jnp.where(marks, jnp.exp(jnp.where(marks, logits - peak, 0.0)), 0.0)
    gates = lifted / jnp.sum(lifted, axis=-1, keepdims=True)
    gates_ref[...] = gates

    arrive(copies, 4, 5)
    for e in range(3):
        for i in range(2):
            cols = slice(i * 256, (i + 1) * 256)
            flat = slice(e * 512 + i * 256, e * 512 + (i + 1) * 256)
            gl = dot(ne_ref[...], wg[e, :, cols], NN)
            ul = dot(ne_ref[...], wu[e, :, cols], NN)
            gl_ref[:, flat] = gl.astype(BF16)
            ul_ref[:, flat] = ul.astype(BF16)
            inner = gl * jax.nn.sigmoid(gl) * ul
            gi_ref[:, flat] = (gates[:, 2 + e:3 + e] * inner).astype(BF16)

    arrive(copies, 6)
    for i in range(4):
        cols = slice(i * 256, (i + 1) * 256)
        total = middle_ref[:, cols]
        for e in range(3):
            total = total + dot(gi_ref[:, e * 512:(e + 1) * 512], wd[e, :, cols], NN)
        out_ref[:, cols] = total
        relay_ref[:, cols] = total.astype(BF16)


KEPT = (
    ((TOKENS, WIDTH), F32), ((TOKENS, WIDTH), BF16), ((TOKENS, WIDTH), BF16), ((TOKENS, WIDTH), BF16),
    ((TOKENS, 512), BF16), ((TOKENS, 512), BF16), ((2, 8, 256, 128), BF16), ((TOKENS, WIDTH), BF16),
    ((TOKENS, WIDTH), F32), ((TOKENS, WIDTH), BF16), ((TOKENS, 16), F32), ((TOKENS, 1536), BF16),
    ((TOKENS, 1536), BF16), ((TOKENS, 1536), BF16),
)


def specs(places):
    return [pl.BlockSpec(memory_space=place) for place in places]


def forward(start, received, bias, marks, cos, sin, small, weights, keep):
    scratch = [pltpu.VMEM(shape, BF16) for shape in WEIGHT_SHAPES] + [pltpu.SemaphoreType.DMA((14,))]
    outs = (((TOKENS, WIDTH), BF16),)
    if keep:
        outs = outs + KEPT
    else:
        scratch = [pltpu.VMEM(shape, kind) for shape, kind in KEPT] + scratch
    return pl.pallas_call(
        forward_kernel,
        out_shape=tuple(jax.ShapeDtypeStruct(shape, kind) for shape, kind in outs),
        in_specs=specs([pltpu.VMEM] * 8 + [pl.ANY] * 14),
        out_specs=tuple(specs([pltpu.VMEM] * len(outs))),
        scratch_shapes=scratch,
        compiler_params=pltpu.CompilerParams(vmem_limit_bytes=VMEM_LIMIT),
    )(start, received, bias, marks, cos, sin, *small, *weights[0], *weights[1])


def norm_back(rows, scale, gain, incoming):
    weighted = incoming * gain
    gain_part = jnp.sum(incoming * rows * scale, axis=0, keepdims=True)
    part = scale * weighted - rows * (scale * scale * scale) * jnp.mean(weighted * rows, axis=-1, keepdims=True)
    return part, gain_part


def backward_kernel(
    returned_ref, cotangent_ref, cos_ref, sin_ref, small_mine, small_other,
    hidden_ref, normed_ref, q_ref, k_ref, v_ref, p_ref, att_ref, middle_ref, ne_ref, gates_ref, gl_ref, ul_ref,
    *refs,
):
    mine, others, refs = refs[:7], refs[7:14], refs[14:]
    relay_ref, grad_ref, small_grad, up_ref, bgu_ref, bb_ref, bqkv_ref = refs[:7]
    held, (sems, bne_ref, bm_ref, ba_ref) = refs[7:14], refs[14:]
    wq, wk, wv, wo, wg, wu, wd = held
    copies = weight_copies(mine, others, held, sems)
    start_all(copies, (6, 4, 5, 3, 0, 1, 2))
    small = small_rows(small_mine, small_other)
    first = lax.axis_index("section") == 0
    up_ref[...] = jnp.where(first, returned_ref[...], cotangent_ref[...])
    gates = gates_ref[...]
    lane = lax.broadcasted_iota(jnp.int32, gates.shape, 1)
    pulls = jnp.zeros_like(gates)

    arrive(copies, 6)
    for e in range(3):
        gate = gates[:, 2 + e:3 + e]
        for i in range(2):
            flat = slice(e * 512 + i * 256, e * 512 + (i + 1) * 256)
            u = dot(up_ref[...], wd[e, i * 256:(i + 1) * 256, :], NT)
            gl = gl_ref[:, flat].astype(F32)
            ul = ul_ref[:, flat].astype(F32)
            sg = jax.nn.sigmoid(gl)
            silu = gl * sg
            pulls = pulls + jnp.where(lane == 2 + e, jnp.sum(u * silu * ul, axis=-1, keepdims=True), 0.0)
            inner = gate * u
            at = e * 1024 + i * 256
            bgu_ref[:, at:at + 256] = (inner * ul * sg * (1.0 + gl * (1.0 - sg))).astype(BF16)
            bgu_ref[:, at + 512:at + 768] = (inner * silu).astype(BF16)
    back_logits = (gates * (pulls - jnp.sum(gates * pulls, axis=-1, keepdims=True))).astype(BF16)

    arrive(copies, 4, 5)
    for i in range(4):
        cols = slice(i * 256, (i + 1) * 256)
        total = dot(back_logits, small[:, cols], NN)
        for e in range(3):
            total = total + dot(bgu_ref[:, e * 1024:e * 1024 + 512], wg[e, cols, :], NT)
            total = total + dot(bgu_ref[:, e * 1024 + 512:e * 1024 + 1024], wu[e, cols, :], NT)
        bne_ref[:, cols] = total
    middle = middle_ref[...]
    part, expert_gain = norm_back(middle, scale_of(middle), small[1:2].astype(F32), bne_ref[...])
    bm_ref[...] = up_ref[...].astype(F32) + part
    bb_ref[...] = bm_ref[...].astype(BF16)

    arrive(copies, 3)
    for i in range(4):
        cols = slice(i * 256, (i + 1) * 256)
        ba_ref[:, cols] = dot(bb_ref[...], wo[cols, :], NT).astype(BF16)

    cos, sin = cos_ref[0:128, 0:128], sin_ref[0:128, 0:128]

    def unturn(u):
        return (u * cos - swap_halves(u) * sin).astype(BF16)

    for pack in range(2):
        rows = slice(pack * 128, pack * 128 + 128)
        for pair in range(4):
            keys = both_ways(k_ref[rows, pair * 128:(pair + 1) * 128])
            values = both_ways(v_ref[rows, pair * 128:(pair + 1) * 128])
            back_k, back_v = [], []
            for half in range(2):
                g = pair * 2 + half
                cols = slice(g * 128, (g + 1) * 128)
                queries = stack_heads(q_ref[rows, cols])
                back_out = stack_heads(ba_ref[rows, cols])
                attention = p_ref[pack, g]
                wide = attention.astype(F32)
                pull = dot(back_out, values[half], NT)
                bv = dot(attention, back_out, TN)
                back_v.append(bv + pltpu.roll(bv, 64, 1))
                spread = wide * pull
                back_scores = (
                    (spread - wide * jnp.sum(spread, axis=-1, keepdims=True)) * 0.125
                ).astype(BF16)
                bqkv_ref[rows, cols] = unturn(join_heads(dot(back_scores, keys[half], NN)))
                bk = dot(back_scores, queries, TN)
                back_k.append(bk + pltpu.roll(bk, 64, 1))
            low = low_half((128, 128))
            at = 1024 + pair * 128
            bqkv_ref[rows, at:at + 128] = unturn(jnp.where(low, back_k[0], back_k[1]))
            bqkv_ref[rows, at + 512:at + 640] = jnp.where(low, back_v[0], back_v[1]).astype(BF16)

    arrive(copies, 0, 1, 2)
    for i in range(4):
        cols = slice(i * 256, (i + 1) * 256)
        total = dot(bqkv_ref[:, 0:1024], wq[cols, :], NT)
        total = total + dot(bqkv_ref[:, 1024:1536], wk[cols, :], NT)
        bne_ref[:, cols] = total + dot(bqkv_ref[:, 1536:2048], wv[cols, :], NT)
    x = hidden_ref[...].astype(F32)
    part, mixer_gain = norm_back(x, scale_of(x), small[0:1].astype(F32), bne_ref[...])
    total = bm_ref[...] + part
    grad_ref[...] = total
    relay_ref[...] = total.astype(BF16)

    router = dot(back_logits, ne_ref[...], TN)
    row = lax.broadcasted_iota(jnp.int32, router.shape, 0)
    mixed = jnp.where(row == 0, mixer_gain, jnp.where(row == 1, expert_gain, router))
    small_grad[0] = mixed[:, 0:512]
    small_grad[1] = mixed[:, 512:1024]


def backward(returned, cotangent, cos, sin, small, kept, weights, keep):
    hidden, normed, q, k, v, p, att, middle, ne, gates, gl, ul, gi = kept
    rest = (
        ((TOKENS, WIDTH), F32), ((2, 16, 512), F32), ((TOKENS, WIDTH), BF16), ((TOKENS, 3072), BF16),
        ((TOKENS, WIDTH), BF16), ((TOKENS, 2048), BF16),
    )
    outs = (((TOKENS, WIDTH), BF16),)
    scratch = [pltpu.VMEM(shape, BF16) for shape in WEIGHT_SHAPES] + [
        pltpu.SemaphoreType.DMA((14,)),
        pltpu.VMEM((TOKENS, WIDTH), F32), pltpu.VMEM((TOKENS, WIDTH), F32), pltpu.VMEM((TOKENS, WIDTH), BF16),
    ]
    if keep:
        outs = outs + rest
    else:
        scratch = [pltpu.VMEM(shape, kind) for shape, kind in rest] + scratch
    return pl.pallas_call(
        backward_kernel,
        out_shape=tuple(jax.ShapeDtypeStruct(shape, kind) for shape, kind in outs),
        in_specs=specs([pltpu.VMEM] * 18 + [pl.ANY] * 14),
        out_specs=tuple(specs([pltpu.VMEM] * len(outs))),
        scratch_shapes=scratch,
        compiler_params=pltpu.CompilerParams(vmem_limit_bytes=VMEM_LIMIT),
    )(returned, cotangent, cos, sin, *small, hidden, normed, q, k, v, p, att, middle, ne, gates, gl, ul,
      *weights[0], *weights[1])


def weight_grad_kernel(normed_ref, att_ref, ne_ref, gi_ref, up_ref, bgu_ref, bb_ref, bqkv_ref, out_ref, held, sems):
    copies = []

    def tile(a, a_at, count, b, b_at, half, at):
        value = dot(a[:, a_at:a_at + count], b[:, b_at:b_at + 512], TN)
        held[half, at:at + count, :] = value.astype(BF16)

    def send(half, at, count):
        place = (half, pl.ds(at, count))
        copy = pltpu.make_async_copy(held.at[place], out_ref.at[place], sems.at[len(copies)])
        copy.start()
        copies.append(copy)

    for half in range(2):
        for i in range(2):
            tile(normed_ref, half * 512, 512, bqkv_ref, i * 512, half, i * 512)
            tile(normed_ref, half * 512, 512, bqkv_ref, 1024 + i * 512, half, 1024 + i * 512)
            tile(att_ref, half * 512, 512, bb_ref, i * 512, half, 2048 + i * 512)
        send(half, 0, 3072)
        for e in range(3):
            for i in range(2):
                tile(ne_ref, half * 512, 512, bgu_ref, e * 1024 + i * 512, half, 3072 + e * 1024 + i * 512)
        send(half, 3072, 3072)
        for e in range(3):
            for i in range(2):
                tile(gi_ref, e * 512 + half * 256, 256, up_ref, i * 512, half, 6144 + e * 512 + i * 256)
        send(half, 6144, 1536)
    for copy in copies:
        copy.wait()


def weight_grads(normed, att, ne, gi, up, bgu, bb, bqkv):
    return pl.pallas_call(
        weight_grad_kernel,
        out_shape=jax.ShapeDtypeStruct((2, ROWS, COLS), BF16),
        in_specs=specs([pltpu.VMEM] * 8),
        out_specs=pl.BlockSpec(memory_space=pl.ANY),
        scratch_shapes=[pltpu.VMEM((2, ROWS, COLS), BF16), pltpu.SemaphoreType.DMA((6,))],
        compiler_params=pltpu.CompilerParams(vmem_limit_bytes=VMEM_LIMIT),
    )(normed, att, ne, gi, up, bgu, bb, bqkv)


def rotary_tables():
    lane = np.arange(256)
    frequency = np.power(10000.0, -2.0 * (lane % 32) / 64.0)
    angles = (np.arange(TOKENS) % 128)[:, None] * frequency[None, :]
    sign = np.where(lane % 64 < 32, -1.0, 1.0)[None, :]
    return np.cos(angles).astype(np.float32), (np.sin(angles) * sign).astype(np.float32)


def body(
    inputs, cotangent, segments, routes, mixer_gain, query_weight, key_matrix, value_matrix, out_weight,
    expert_gain, router_weight, gate_weight, up_weight, down_weight,
):
    start = inputs.reshape(TOKENS, WIDTH)
    loss = cotangent.reshape(TOKENS, WIDTH)
    small_mine = jnp.concatenate(
        [mixer_gain, expert_gain, jnp.transpose(router_weight[0]), jnp.zeros((11, 512), BF16)], axis=0
    )
    mine = (
        query_weight[0], key_matrix[0], value_matrix[0], out_weight[0], gate_weight[0], up_weight[0],
        down_weight[0],
    )
    *others, small_other = exchange(*mine, small_mine)
    weights = (mine, tuple(others))
    small = (small_mine, small_other)
    seg = segments[:, 0]
    place = jnp.arange(128, dtype=jnp.int32)
    allowed = (seg[:, :, None] == seg[:, None, :]) & (place[None, None, :] <= place[None, :, None])
    bias = jnp.where(allowed, 0.0, -1e30).astype(F32)
    picks = routes.reshape(TOKENS, 2)
    columns = jnp.arange(16, dtype=jnp.int32)[None, :] - 2
    marks = ((picks[:, 0:1] == columns) | (picks[:, 1:2] == columns)).astype(F32)
    cos, sin = (jnp.asarray(table) for table in rotary_tables())

    (relay,) = forward(start, start, bias, marks, cos, sin, small, weights, False)
    received = lax.ppermute(relay, "section", [(0, 1)])
    relay, out, *kept = forward(start, received, bias, marks, cos, sin, small, weights, True)
    (relay,) = backward(loss, loss, cos, sin, small, kept, weights, False)
    returned = lax.ppermute(relay, "section", [(1, 0)])
    relay, grad, small_grad, up, bgu, bb, bqkv = backward(
        returned, loss, cos, sin, small, kept, weights, True
    )
    parts = weight_grads(kept[1], kept[6], kept[8], kept[12], up, bgu, bb, bqkv)
    total, small_total = reduce_gradients(parts, small_grad)

    def wide(at, rows):
        return jnp.concatenate([total[at:at + rows], total[at + rows:at + 2 * rows]], axis=1).astype(F32)

    experts = total[3072:6144].reshape(3, 2, 512, 512).astype(F32)
    down = total[6144:7680].reshape(3, 2, 256, 512)
    down = jnp.concatenate([down[:, 0], down[:, 1]], axis=-1).astype(F32)
    return (
        out.reshape(1, 2, 1, 128, WIDTH),
        grad.reshape(1, 2, 1, 128, WIDTH),
        small_total[0:1],
        wide(0, 512)[None],
        total[1024:1536].astype(F32)[None],
        total[1536:2048].astype(F32)[None],
        wide(2048, 512)[None],
        small_total[1:2],
        jnp.transpose(small_total[2:5])[None],
        experts[:, 0][None],
        experts[:, 1][None],
        down[None],
    )


def solution(mesh):
    return jax.shard_map(
        body,
        mesh=mesh,
        in_specs=(
            P(None, ("shard", "replica"), None, None),
            P(None, ("shard", "replica"), None, None),
            P(None, ("shard", "replica"), None),
            P("section", None, ("shard", "replica"), None, None),
            P("section", "shard"),
            P("section", "shard", None),
            P("section", "shard", None),
            P("section", "shard", None),
            P("section", "shard", None),
            P("section", "shard"),
            P("section", "shard", None),
            P("section", None, "shard", None),
            P("section", None, "shard", None),
            P("section", None, "shard", None),
        ),
        out_specs=(
            P("section", None, ("shard", "replica"), None, None),
            P("section", None, ("shard", "replica"), None, None),
            P("section", "shard"),
            P("section", "shard", None),
            P("section", "shard", None),
            P("section", "shard", None),
            P("section", "shard", None),
            P("section", "shard"),
            P("section", "shard", None),
            P("section", None, "shard", None),
            P("section", None, "shard", None),
            P("section", None, "shard", None),
        ),
        check_vma=False,
    )
```

time: 785 us -> 256 us (0.33)
  waiting for transfers between devices: 427 us -> 27 us
  Pallas kernels: 0 us -> 196 us
  matrix products: 141 us -> 0 us
  blocking collectives: 92.4 us -> 0 us
  other arithmetic: 47.7 us -> 12.9 us
  local copies, waits for them, and re-layouts: 35 us -> 10.9 us
  between operations: 18 us -> 1 us
  starting transfers between devices: 15.6 us -> 6.77 us
    psum x1 -> x0, waiting for transfers between devices: 260 us -> none  [body(): lax.psum(owned[1].astype(jnp.bfloat16), 'replica').astype(jnp.float32)]
    pallas_call x0 -> x7, Pallas kernels: none -> 196 us  [the longest x1 101 us: reduce_gradients(): pl.pallas_call(reduce_kernel, out_shape=(jax.ShapeDtypeStruct((ROWS, COLS...]
    dot_general x102 -> x0, matrix products: 141 us -> none  [the longest x3 11.2 us: layer_backward(): jnp.einsum('sd,se->de', normalized_input, back_queries, preferred_element...]
    psum x1 -> x0, blocking collectives: 84.6 us -> none  [body(): lax.psum(owned[0].astype(jnp.bfloat16), 'replica').astype(jnp.float32)]
    all_gather x7 -> x0, waiting for transfers between devices: 78.8 us -> none  [the longest x1 15.1 us: collect(): lax.all_gather(local[8], 'shard', axis=1, tiled=True)]
    reduce_scatter x7 -> x0, waiting for transfers between devices: 61.4 us -> none  [the longest x1 18 us: body(): lax.psum_scatter(totals[7].astype(jnp.bfloat16), 'shard', scatter_dimensi...]
    unnamed x420 -> x7, local copies, waits for them, and re-layouts: 21 us -> 2.22 us
    broadcast_in_dim x9 -> x0, other arithmetic: 14.1 us -> none  [body(): piece[None]]
  transfers between devices with their start and end apart: 20 -> 2, of which waited for: 16 -> 2; matrix products, arithmetic and copies ran while one was open for 12% -> 0% of each run, Pallas kernels for 0% -> 0%
where the time goes in v1:
time: 256 us; the launch traced here: 255 us
  Pallas kernels  196 us (77%)
  waiting for transfers between devices  27 us (11%)
  other arithmetic  12.9 us (5%)
  local copies, waits for them, and re-layouts  10.9 us (4%)
  starting transfers between devices  6.77 us (3%)
    pallas_call x1, Pallas kernels, reduce_gradients(): pl.pallas_call(reduce_kernel, out_shape=(jax.ShapeDtypeStruct((ROWS, COLS...  101 us
    pallas_call x2, Pallas kernels, backward(): pl.pallas_call(backward_kernel, out_shape=tuple((jax.ShapeDtypeStruct(sha...  47.5 us
    pallas_call x2, Pallas kernels, forward(): pl.pallas_call(forward_kernel, out_shape=tuple((jax.ShapeDtypeStruct(shap...  25.9 us
    ppermute x1, waiting for transfers between devices, body(): returned = lax.ppermute(relay, 'section', [(1, 0)])  15.5 us
    pallas_call x1, Pallas kernels, exchange(): pl.pallas_call(functools.partial(gather_kernel, n), out_shape=tuple((jax....  12.9 us
    ppermute x1, waiting for transfers between devices, body(): received = lax.ppermute(relay, 'section', [(0, 1)])  11.5 us
    pallas_call x1, Pallas kernels, weight_grads(): pl.pallas_call(weight_grad_kernel, out_shape=jax.ShapeDtypeStruct((2, ROW...  9.34 us
    ppermute x1, starting transfers between devices, body(): received = lax.ppermute(relay, 'section', [(0, 1)])  5.48 us
  transfers between devices with their start and end apart: 2, of which 2 were waited for; matrix products, arithmetic and copies ran while one was open for 0% of the time, Pallas kernels for 0%

profile of v1, /device:TPU:0, one launch (start us, length us, event | category | flops | bytes accessed | tf_op | source)
XLA Modules:
  0.0 254.7 jit_solution(10342095088160788505)
XLA Ops:
  0.7 0.8 fusion.1
  1.4 0.1 pad.9.clone
  1.5 1.5 and_select_fusion.bias_ref
  3.0 0.8 or_convert_fusion.marks_ref
  3.8 1.4 maximum_maximum_fusion.refs_7_.small_mine
  5.2 12.9 %shard_map.247 = (bf16[512,1024]{1,0:T(8,128)(2,1)}, bf16[512,512]{1,0:T(8,128)(2,1)}, bf16[512,512]{1,0:T(8,128)(2,1)}, bf16[512,1024]{1,0:T(8,128)(2,1)}, bf16...) custom-call(bf16[512,1024]{1,0:T(8,128)(2,1)} %bitcast.74, ...), custom_call_target="tpu_custom_call" | custom-call | tf_op jit(solution)/shard_map/pallas_call | solution.py:242
  18.1 12.1 %shard_map.248 = bf16[256,1024]{1,0:T(8,128)(2,1)} custom-call(bf16[256,1024]{1,0:T(8,128)(2,1)} %bitcast.96, bf16[256,1024]{1,0:T(8,128)(2,1)} %bitcast.97, f32[2,128,128]{2,1,0:T(8,128)} %and_select_fusion.bias_ref, f32[256,16]{1,0:T(8,128)} %or_convert_fusion.marks_ref, f32[256,256]{1,0:T(8,128)} %constant.13.clone.cos_ref, ...), custom_call_target="tpu_custom_call" | custom-call | tf_op jit(solution)/shard_map/pallas_call | solution.py:435
  30.3 5.5 %collective-permute-start = (bf16[256,1024]{1,0:T(8,128)(2,1)}, bf16[256,1024]{1,0:T(8,128)(2,1)S(1)}, u32[]{:S(2)}, u32[]{:S(2)}) collective-permute-start(bf16[256,1024]{1,0:T(8,128)(2,1)} %shard_map.248), channel_id=1, source_target_pairs={{0,64},{1,65},{2,66},{3,67},{4,68},{5,69},{6,70},{7,71},{8,72},{9,... | collective-permute-start | bytes 1572872 | tf_op jit(solution)/shard_map/ppermute | solution.py:659
  35.8 11.5 %collective-permute-done.received_ref = bf16[256,1024]{1,0:T(8,128)(2,1)S(1)} collective-permute-done((bf16[256,1024]{1,0:T(8,128)(2,1)}, bf16[256,1024]{1,0:T(8,128)(2,1)S(1)}, u32[]{:S(2)}, u32[]{:S(2)}) %collective-permute-start) | collective-permute-done | bytes 524320 | tf_op jit(solution)/shard_map/ppermute | solution.py:659
  47.3 0.0 copy-start.2
  47.3 0.8 copy-done.2
  48.0 13.8 %shard_map.249 = (bf16[256,1024]{1,0:T(8,128)(2,1)}, f32[256,1024]{1,0:T(8,128)}, bf16[256,1024]{1,0:T(8,128)(2,1)}, bf16[256,1024]{1,0:T(8,128)(2,1)}, bf16[256...) custom-call(bf16[256,1024]{1,0:T(8,128)(2,1)} %bitcast.98, ...), custom_call_target="tpu_custom_call" | custom-call | tf_op jit(solution)/shard_map/pallas_call | solution.py:435
  61.8 29.3 %shard_map.250 = bf16[256,1024]{1,0:T(8,128)(2,1)} custom-call(bf16[256,1024]{1,0:T(8,128)(2,1)} %bitcast.99, bf16[256,1024]{1,0:T(8,128)(2,1)} %bitcast.100, f32[256,256]{1,0:T(8,128)} %constant.13.clone.cos_ref, f32[256,256]{1,0:T(8,128)} %constant.14.clone.sin_ref, bf16[16,512]{1,0:T(8,128)(2,1)} %maximum_maximum_fusion.refs_7_.small_mine, ...), custom_call_target="tpu_custom_call" | custom-call | tf_op jit(solution)/shard_map/pallas_call | solution.py:572
  91.2 1.3 collective-permute-start.1
  92.5 15.5 %collective-permute-done.1.returned_ref = bf16[256,1024]{1,0:T(8,128)(2,1)S(1)} collective-permute-done((bf16[256,1024]{1,0:T(8,128)(2,1)}, bf16[256,1024]{1,0:T(8,128)(2,1)S(1)}, u32[]{:S(2)}, u32[]{:S(2)}) %collective-permute-start.1) | collective-permute-done | bytes 524320 | tf_op jit(solution)/shard_map/ppermute | solution.py:662
  107.9 0.0 copy-start.1
  107.9 0.8 copy-done.1
  108.7 18.2 %shard_map.251 = (bf16[256,1024]{1,0:T(8,128)(2,1)}, f32[256,1024]{1,0:T(8,128)}, f32[2,16,512]{2,1,0:T(8,128)}, bf16[256,1024]{1,0:T(8,128)(2,1)}, bf16[256,307...) custom-call(bf16[256,1024]{1,0:T(8,128)(2,1)} %copy-done.1, bf16[256,1024]{1,0:T(8,128)(2,1)} %bitcast.101, ...), custom_call_target="tpu_custom_call" | custom-call | tf_op jit(solution)/shard_map/pallas_call | solution.py:572
  127.0 0.0 copy-start
  127.0 9.3 %shard_map.252.parts_ref = bf16[2,7680,512]{2,1,0:T(8,128)(2,1)} custom-call(bf16[256,1024]{1,0:T(8,128)(2,1)} %get-tuple-element.52.normed_ref, bf16[256,1024]{1,0:T(8,128)(2,1)} %get-tuple-element.57.att_ref, bf16[256,1024]{1,0:T(8,128)(2,1)} %get-tuple-element.59.ne_ref, bf16[256,1536]{1,0:T(8,128)(2,1)} %get-tuple-element.64.gi_ref, ...), custom_call_target="tpu_custom_call" | custom-call | tf_op jit(solution)/shard_map/pallas_call | solution.py:615
  136.3 0.0 copy-done
  136.4 100.5 %shard_map.253 = (bf16[7680,512]{1,0:T(8,128)(2,1)}, f32[16,512]{1,0:T(8,128)S(1)}) custom-call(bf16[2,7680,512]{2,1,0:T(8,128)(2,1)} %shard_map.252.parts_ref, f32[2,16,512]{2,1,0:T(8,128)S(1)} %copy-done), custom_call_target="tpu_custom_call" | custom-call | tf_op jit(solution)/shard_map/pallas_call | solution.py:193
  236.9 0.6 fusion
  237.5 1.5 slice.65
  239.0 2.1 slice.62
  241.1 3.6 %slice_bitcast_fusion.5 = (bf16[1,512,512]{2,1,0:T(8,128)(2,1)S(1)}, bf16[1,512,512]{2,1,0:T(8,128)(2,1)S(1)}, f32[1,512,512]{2,1,0:T(8,128)}, f32[1,512,512]{2,...) fusion(bf16[7680,512]{1,0:T(8,128)(2,1)} %get-tuple-element.71), kind=kLoop, calls=%fused_computation.10 | loop fusion | flops 524288 | bytes 7340032 | tf_op jit(solution)/shard_map/concatenate | solution.py:670
  244.7 0.6 copy.49
  245.3 0.2 slice_bitcast_fusion.3
  245.5 0.9 convert.5
  246.3 3.4 %slice_bitcast_fusion = (f32[1,3,512,512]{3,2,1,0:T(8,128)}, f32[1,3,512,512]{3,2,1,0:T(8,128)}) fusion(f32[3,2,512,512]{3,2,1,0:T(8,128)S(1)} %convert.5), kind=kLoop, calls=%fused_computation | loop fusion | bytes 12582912 | tf_op jit(solution)/shard_map/broadcast_in_dim;squeeze | solution.py:686
  249.7 2.1 maximum_convert_fusion
  251.8 2.6 %maximum_convert_fusion.1 = (f32[1,512,1024]{2,1,0:T(8,128)}, f32[1,512,1024]{2,1,0:T(8,128)}) fusion(bf16[1,512,512]{2,1,0:T(8,128)(2,1)S(1)} %get-tuple-element.112, bf16[1,512,512]{2,1,0:T(8,128)(2,1)S(1)} %get-tuple-element.113, bf16[1,512,512]{2,1,0:T(8,128)(2,1)S(1)} %get-tuple-element.109, bf16[1,512,512]{2,1,0:T(8,128)(2,1)S(1)} %get-tuple-element.108), kind=kLoop, calls=%fused_computation.3 | loop fusion | flops 4194304 | bytes 6291456 | tf_op jit(solution)/shard_map/convert_element_type | solution.py:670
  (4 shorter events, 0.0 us)
Async XLA Ops:
  30.3 17.0 %collective-permute-start = (bf16[256,1024]{1,0:T(8,128)(2,1)}, bf16[256,1024]{1,0:T(8,128)(2,1)S(1)}, u32[]{:S(2)}, u32[]{:S(2)}) collective-permute-start(bf16[256,1024]{1,0:T(8,128)(2,1)} %shard_map.248), channel_id=1, source_target_pairs={{0,64},{1,65},{2,66},{3,67},{4,68},{5,69},{6,70},{7,71},{8,72},{9,... | collective-permute-start | bytes 1572872 | tf_op jit(solution)/shard_map/ppermute | solution.py:659
  47.3 0.8 copy-start.2
  91.2 16.8 %collective-permute-start.1 = (bf16[256,1024]{1,0:T(8,128)(2,1)}, bf16[256,1024]{1,0:T(8,128)(2,1)S(1)}, u32[]{:S(2)}, u32[]{:S(2)}) collective-permute-start(bf16[256,1024]{1,0:T(8,128)(2,1)} %shard_map.250), channel_id=1, source_target_pairs={{64,0},{65,1},{66,2},{67,3},{68,4},{69,5},{70,6},{71,7},{72,8},{73... | collective-permute-start | bytes 1572872 | tf_op jit(solution)/shard_map/ppermute | solution.py:662
  107.9 0.8 copy-start.1
  127.0 9.4 %copy-start = (f32[2,16,512]{2,1,0:T(8,128)S(1)}, f32[2,16,512]{2,1,0:T(8,128)}, u32[]{:S(2)}) copy-start(f32[2,16,512]{2,1,0:T(8,128)} %get-tuple-element.69.small_ref) | copy-start | bytes 196612
